TPU v7x, 128 devices: a whole 4x4x4 slice. The times are simulated.
128 devices in a mesh: gx: 16 (over z, x), gy: 2 (over y_lo), gz: 4 (over y_hi, core).
Axes of the slice: x: 4, y: 4 (y_hi: 2, y_lo: 2; y = y_hi * 2 + y_lo), z: 4, core: 2. Of those that a mesh axis runs over, the one named last changes fastest.
Arguments:
- tensor: float32 [512, 768, 512], P('gx', 'gy', 'gz'), may hold values from -12 to 12
- factor_b: float32 [768, 64], P(('gy', 'gx', 'gz')), may hold values from -8 to 8
- factor_c: float32 [512, 64], P(('gz', 'gx', 'gy')), may hold values from -8 to 8
Outputs:
- factor_a_out: float32 [512, 64], P(('gx', 'gy', 'gz'))
- factor_b_out: float32 [768, 64], P(('gy', 'gx', 'gz'))
- factor_c_out: float32 [512, 64], P(('gz', 'gx', 'gy'))
All inputs are finite; a program needn't handle non-finite values.
Results may differ from a plain program's by a relative error of at most 0.0007.
Values sent between devices are 32-bit elements; how exact they have to be, the bound alone decides.
A program may use at most 64 MiB of HBM per device.

v0:
```python
import jax
import jax.numpy as jnp
from jax import lax
from jax.sharding import PartitionSpec as P

HIGHEST_PRECISION = lax.Precision.HIGHEST


def solve_rows(moment, system):
    lower = jnp.linalg.cholesky(system)
    halfway = lax.linalg.triangular_solve(
        lower, moment, left_side=False, lower=True, transpose_a=True
    )
    return lax.linalg.triangular_solve(
        lower, halfway, left_side=False, lower=True, transpose_a=False
    )


def settle(unscaled, gram_raw, total_rows):
    scales = jnp.sqrt(jnp.diagonal(gram_raw) / total_rows + 1e-06)
    return (unscaled / scales[None, :], gram_raw / (scales[:, None] * scales[None, :]))


def gram_of(factor):
    return jnp.dot(
        factor.T, factor, precision=HIGHEST_PRECISION, preferred_element_type=jnp.float32
    )


def local(tensor, factor_b, factor_c):
    span_i, span_j, span_k = tensor.shape
    total_i = span_i * lax.axis_size("gx")
    total_j = span_j * lax.axis_size("gy")
    total_k = span_k * lax.axis_size("gz")
    gram_b, gram_c = lax.psum((gram_of(factor_b), gram_of(factor_c)), ("gx", "gy", "gz"))
    block_b = lax.all_gather(factor_b, ("gx", "gz"), axis=0, tiled=True)
    block_c = lax.all_gather(factor_c, ("gx", "gy"), axis=0, tiled=True)
    along_k = jnp.einsum("ijk,kr->rij", tensor, block_c, precision=HIGHEST_PRECISION)
    window = along_k
    moment = lax.psum_scatter(
        jnp.einsum("rij,jr->ir", window, block_b, precision=HIGHEST_PRECISION),
        ("gy", "gz"),
        scatter_dimension=0,
        tiled=True,
    )
    unscaled = solve_rows(moment, gram_b * gram_c)
    gram_raw = lax.psum(gram_of(unscaled), ("gx", "gy", "gz"))
    shard_a, gram_a = settle(unscaled, gram_raw, total_i)
    block_a = lax.all_gather(shard_a, ("gy", "gz"), axis=0, tiled=True)
    window = along_k
    moment = lax.psum_scatter(
        jnp.einsum("rij,ir->jr", window, block_a, precision=HIGHEST_PRECISION),
        ("gx", "gz"),
        scatter_dimension=0,
        tiled=True,
    )
    unscaled = solve_rows(moment, gram_a * gram_c)
    gram_raw = lax.psum(gram_of(unscaled), ("gx", "gy", "gz"))
    shard_b, gram_b = settle(unscaled, gram_raw, total_j)
    block_b = lax.all_gather(shard_b, ("gx", "gz"), axis=0, tiled=True)
    along_j = jnp.einsum("ijk,ir->rjk", tensor, block_a, precision=HIGHEST_PRECISION)
    window = along_j
    moment = lax.psum_scatter(
        jnp.einsum("rjk,jr->kr", window, block_b, precision=HIGHEST_PRECISION),
        ("gx", "gy"),
        scatter_dimension=0,
        tiled=True,
    )
    unscaled = solve_rows(moment, gram_a * gram_b)
    gram_raw = lax.psum(gram_of(unscaled), ("gx", "gy", "gz"))
    shard_c, gram_c = settle(unscaled, gram_raw, total_k)
    return (shard_a, shard_b, shard_c)


def solution(mesh):
    return jax.shard_map(
        local,
        mesh=mesh,
        in_specs=(P("gx", "gy", "gz"), P(("gy", "gx", "gz"), None), P(("gz", "gx", "gy"), None)),
        out_specs=(
            P(("gx", "gy", "gz"), None),
            P(("gy", "gx", "gz"), None),
            P(("gz", "gx", "gy"), None),
        ),
        check_vma=False,
    )
```

profile of v0, /device:TPU:1, one launch (start us, length us, event | category | flops | bytes accessed | tf_op | source)
XLA Modules:
  0.0 1361.7 jit_solution(8903045600152034252)
XLA Ops:
  7.2 1.0 fusion.29
  8.2 1.0 fusion.30
  9.2 69.2 %all-reduce.3 = (f32[64,64]{0,1:T(8,128)S(1)}, f32[64,64]{0,1:T(8,128)S(1)}) all-reduce(f32[64,64]{0,1:T(8,128)S(1)} %fusion.29, f32[64,64]{0,1:T(8,128)S(1)} %fusion.30), channel_id=1, replica_groups=mesh['gx'=16,'gy'=2,'gz'=4] {'gx','gy','gz'}, use_global_device_ids=true, to_apply=%region_0.0 | all-reduce | flops 8192 | bytes 65536 | tf_op jit(solution)/shard_map/psum | solution.py:35
  78.5 5.8 cholesky.59
  84.4 0.6 compare_reduce_fusion.2
  85.0 0.7 fusion.8
  85.7 4.9 custom-call.23
  90.6 63.6 %all-gather = f32[32,4,64]{2,1,0:T(4,128)S(1)} all-gather(f32[1,4,64]{2,1,0:T(4,128)} %bitcast.107), channel_id=1, replica_groups=mesh['gx'=16,'gy'=2,'gz'=4] {'gx','gy'}, dimensions={0}, use_global_device_ids=true | all-gather | bytes 33792 | tf_op jit(solution)/shard_map/all_gather | solution.py:37
  154.2 106.6 %all-gather.1 = f32[64,6,64]{2,1,0:T(8,128)S(1)} all-gather(f32[1,6,64]{2,1,0:T(8,128)} %bitcast.106), channel_id=1, replica_groups=mesh['gx'=16,'gy'=2,'gz'=4] {'gx','gz'}, dimensions={0}, use_global_device_ids=true | all-gather | bytes 99840 | tf_op jit(solution)/shard_map/all_gather | solution.py:36
  260.9 8.9 fusion.31
  269.8 5.2 fusion.6
  275.0 24.1 %all-reduce = f32[32,64]{0,1:T(8,128)S(1)} all-reduce(f32[32,64]{0,1:T(8,128)S(1)} %bitcast.105), channel_id=2, replica_groups=mesh['gx'=16,'gy'=2,'gz'=4] {'gy','gz'}, use_global_device_ids=true, to_apply=%region_4.6.clone | all-reduce | flops 2048 | bytes 16384
  301.1 63.3 %psum.37 = f32[64,64]{0,1:T(8,128)S(1)} all-reduce(f32[64,64]{0,1:T(8,128)S(1)} %fusion.32), channel_id=1, replica_groups=mesh['gx'=16,'gy'=2,'gz'=4] {'gx','gy','gz'}, use_global_device_ids=true, to_apply=%region_5.9 | all-reduce | flops 4096 | bytes 32768 | tf_op jit(solution)/shard_map/psum | solution.py:47
  364.3 0.8 gather_fusion
  365.2 13.5 all-gather.2
  378.8 3.6 fusion.4
  383.2 20.6 %fusion.2 = f32[64,384,128]{2,0,1:T(8,128)} fusion(f32[32,64,1]{1,0,2:T(8,128)S(1)} %bitcast.103, f32[32,384,128]{2,1,0:T(8,128)} %param.8), kind=kOutput, calls=%fused_computation.5 | convolution fusion | flops 1207959552 | bytes 18882560 | tf_op jit(solution)/shard_map/ijk,ir->rjk/dot_general | solution.py:61
  403.9 5.8 cholesky.70
  410.4 0.7 fusion.9
  413.5 4.9 custom-call.13
  419.1 523.8 %all-reduce.6.cloned.1.call-done = f32[384,64]{0,1:T(8,128)} async-done(((f32[384,64]{0,1:T(8,128)}), f32[384,64]{0,1:T(8,128)}) %all-reduce.6.cloned.1.call-update) | async-done | bytes 98320
  942.9 1.1 fusion.12
  944.4 65.7 %psum.38 = f32[64,64]{0,1:T(8,128)S(1)} all-reduce(f32[64,64]{0,1:T(8,128)S(1)} %fusion.33), channel_id=1, replica_groups=mesh['gx'=16,'gy'=2,'gz'=4] {'gx','gy','gz'}, use_global_device_ids=true, to_apply=%region_7.11 | all-reduce | flops 4096 | bytes 32768 | tf_op jit(solution)/shard_map/psum | solution.py:58
  1010.1 0.8 gather_fusion.1
  1011.7 5.8 cholesky.81
  1018.3 0.7 fusion.10
  1018.9 4.9 custom-call.25
  1023.8 92.3 %all-gather.3 = f32[64,6,64]{2,1,0:T(8,128)S(1)} all-gather(f32[1,6,64]{2,1,0:T(8,128)S(1)} %fusion.54), channel_id=1, replica_groups=mesh['gx'=16,'gy'=2,'gz'=4] {'gx','gz'}, dimensions={0}, use_global_device_ids=true | all-gather | bytes 99840 | tf_op jit(solution)/shard_map/all_gather | solution.py:60
  1116.3 21.7 %fusion = f32[64,1,128]{2,1,0:T(1,128)S(1)} fusion(f32[384,64,1]{0,2,1:T(1,128)S(1)} %copy.41, f32[64,384,128]{2,0,1:T(8,128)} %fusion.2), kind=kOutput, calls=%fused_computation.3 | convolution fusion | flops 37748736 | bytes 12713984 | tf_op jit(solution)/shard_map/rjk,jr->kr/dot_general | solution.py:64
  1137.9 125.5 %all-reduce.2 = f32[128,64]{0,1:T(8,128)S(1)} all-reduce(f32[128,64]{0,1:T(8,128)S(1)} %bitcast.104), channel_id=4, replica_groups=mesh['gx'=16,'gy'=2,'gz'=4] {'gx','gy'}, use_global_device_ids=true, to_apply=%region_8.12.clone | all-reduce | flops 8192 | bytes 65536
  1264.1 89.1 %psum.39 = f32[64,64]{1,0:T(8,128)S(1)} all-reduce(f32[64,64]{1,0:T(8,128)S(1)} %fusion.34), channel_id=1, replica_groups=mesh['gx'=16,'gy'=2,'gz'=4] {'gx','gy','gz'}, use_global_device_ids=true, to_apply=%region_9.13 | all-reduce | flops 4096 | bytes 32768 | tf_op jit(solution)/shard_map/psum | solution.py:70
  1353.2 0.8 gather_fusion.2
  (48 shorter events, 8.3 us)
Async XLA Ops:
  7.2 935.7 %all-reduce.6.cloned.1.call-start = ((), (), s32[]{:S(2)}) async-start(), calls=%async_computation | async-start | bytes 196608
  260.9 38.2 %copy-start.2 = (u32[128]{0:T(128)S(1)}, u32[128]{0:T(128)}, u32[]{:S(2)}) copy-start(u32[128]{0:T(128)} %constant.102) | copy-start | bytes 1540
  383.1 28.5 %copy-start.1 = (u32[128]{0:T(128)S(1)}, u32[128]{0:T(128)}, u32[]{:S(2)}) copy-start(u32[128]{0:T(128)} %constant.110) | copy-start | bytes 1540
  383.1 29.8 %copy-start = (u32[128]{0:T(128)S(1)}, u32[128]{0:T(128)}, u32[]{:S(2)}) copy-start(u32[128]{0:T(128)} %constant.106) | copy-start | bytes 1540
Sparse Core Ops, SparseCore 0:
  383.2 559.6 all-reduce.5
where the time goes:
time: 1370 us; the launch traced here: 1360 us
  blocking collectives  713 us (52%)
  waiting for transfers between devices  524 us (38%)
  matrix products  64.9 us (5%)
  other arithmetic  38.3 us (3%)
  between operations  16.5 us (1%)
    unnamed x2, waiting for transfers between devices  524 us
    psum x3, blocking collectives, local(): gram_raw = lax.psum(gram_of(unscaled), ('gx', 'gy', 'gz'))  218 us
    unnamed x2, blocking collectives  150 us
    all_gather x1, blocking collectives, local(): block_b = lax.all_gather(factor_b, ('gx', 'gz'), axis=0, tiled=True)  107 us
    all_gather x1, blocking collectives, local(): block_b = lax.all_gather(shard_b, ('gx', 'gz'), axis=0, tiled=True)  92.3 us
    psum x1, blocking collectives, local(): lax.psum((gram_of(factor_b), gram_of(factor_c)), ('gx', 'gy', 'gz'))  69.2 us
    all_gather x1, blocking collectives, local(): block_c = lax.all_gather(factor_c, ('gx', 'gy'), axis=0, tiled=True)  63.6 us
  transfers between devices with their start and end apart: 1, of which 1 were waited for; matrix products, arithmetic and copies ran while one was open for 3% of the time, Pallas kernels for 0%

commit v1 on v0

v1 whole, which is shorter than its diff:
```python
import jax
import jax.numpy as jnp
from jax import lax
from jax.experimental import pallas as pl
from jax.experimental.pallas import tpu as pltpu
from jax.sharding import PartitionSpec as P

MESH = pl.DeviceIdType.MESH
HIGHEST = lax.Precision.HIGHEST
F32 = jnp.float32
BF16 = jnp.bfloat16

RANK = 64
GROUP = 4


def low(shape):
    return lax.broadcasted_iota(jnp.int32, shape, 1) < RANK


def swap(x):
    return pltpu.roll(x, RANK, 1)


def fold(x):
    return x + swap(x)


def compact(x):
    half = x.shape[0] // 2
    return jnp.where(low((half, 128)), x[:half], x[half:])


def expand(x):
    other = swap(x)
    side = low(x.shape)
    return jnp.concatenate([jnp.where(side, x, other), jnp.where(side, other, x)], axis=0)


def block_diagonal(x):
    side = low(x.shape)
    return jnp.concatenate([jnp.where(side, x, 0.0), jnp.where(side, 0.0, x)], axis=0)


def matmul(a, b):
    return jnp.dot(a, b, precision=HIGHEST, preferred_element_type=F32)


def gram_packed(x):
    full = matmul(x.T, x)
    own = jnp.where(low((RANK, 128)), full[:RANK] + swap(full[RANK:]), 0.0)
    return fold(own)


def scale_rows(gram, rows):
    r = lax.broadcasted_iota(jnp.int32, (RANK, 128), 0)
    c = lax.broadcasted_iota(jnp.int32, (RANK, 128), 1)
    both = jnp.where((c == r) | (c == r + RANK), gram, 0.0)
    across = jnp.sum(both, axis=0, keepdims=True)
    down = jnp.sum(jnp.where(c < RANK, both, 0.0), axis=1, keepdims=True)
    return jnp.sqrt(across / rows + 1e-06), jnp.sqrt(down / rows + 1e-06)


def inverse(system):
    lane = lax.broadcasted_iota(jnp.int32, (8, 128), 1) % RANK
    row = lax.broadcasted_iota(jnp.int32, (8, 128), 0)
    rest_lane = lax.broadcasted_iota(jnp.int32, (RANK - 8, 128), 1) % RANK

    def step(_, v):
        cols = [jnp.broadcast_to(v[:, c : c + 1], (RANK, 128)) for c in range(8)]
        diag = [col[:8] for col in cols]
        top = jnp.where(lane < 8, jnp.where(lane == row, 1.0, 0.0), v[:8])
        for c in range(8):
            pivot = 1.0 / jnp.broadcast_to(diag[c][c : c + 1], (8, 128))
            here = row == c
            factor = diag[c]
            line = jnp.broadcast_to(top[c : c + 1], (8, 128)) * pivot
            top = jnp.where(here, line, top - factor * line)
            for d in range(c + 1, 8):
                line = jnp.broadcast_to(diag[d][c : c + 1], (8, 128)) * pivot
                diag[d] = jnp.where(here, line, diag[d] - factor * line)
        rest = jnp.where(rest_lane < 8, 0.0, v[8:])
        for c in range(8):
            rest = rest - cols[c][8:] * jnp.broadcast_to(top[c : c + 1], (RANK - 8, 128))
        return pltpu.roll(jnp.concatenate([rest, top], axis=0), 128 - 8, 1)

    return lax.fori_loop(0, 8, step, system)


def split(x):
    high = x.astype(BF16)
    return high, (x - high.astype(F32)).astype(BF16)


def kernel(
    t_ref, fb_ref, fc_ref, a_ref, b_ref, c_ref,
    t32, thi, tlo, along, weights,
    c_one, c_all, b_one, b_all, b_packed,
    gb_slots, gc_slots, ma_part, ma_slots, ua_slots, ua_rows, a_columns,
    mb_part, mb_slots, mb_sum, ub, gu_slots, mc_part, mc_slots, mc_sum, ss_slots,
    t_sem, send, recv,
):
    gx, gy, gz = lax.axis_index("gx"), lax.axis_index("gy"), lax.axis_index("gz")
    z, x = gx // 4, lax.rem(gx, 4)
    yh, core = gz // 2, lax.rem(gz, 2)
    span_i = t_ref.shape[0]

    def ring(me, size, place):
        return me, [place(lax.rem(me + d, size)) for d in range(1, size)]

    gy_me, gy_peers = ring(gy, 2, lambda p: (gx, p, gz))
    gz_me, gz_peers = ring(gz, 4, lambda p: (gx, gy, p))
    gx_me, gx_peers = ring(gx, 16, lambda p: (p, gy, gz))
    yc_me, yc_peers = ring(gy * 4 + gz, 8, lambda p: (gx, p // 4, lax.rem(p, 4)))
    xc_me, xc_peers = ring(x * 2 + core, 8, lambda p: (z * 4 + p // 2, gy, yh * 2 + lax.rem(p, 2)))
    zh_me, zh_peers = ring(z * 2 + yh, 8, lambda p: ((p // 2) * 4 + x, gy, lax.rem(p, 2) * 2 + core))
    xx_me, xx_peers = ring(x, 4, lambda p: (z * 4 + p, gy, gz))
    zl_me, zl_peers = ring(z * 2 + gy, 8, lambda p: ((p // 2) * 4 + x, lax.rem(p, 2), gz))
    xg_me, xg_peers = ring(x * 4 + gz, 16, lambda p: (z * 4 + p // 4, gy, lax.rem(p, 4)))

    pending = []
    used = [0]

    def start(peers, source, target):
        copies = []
        for d, peer in enumerate(peers):
            at = used[0]
            used[0] += 1
            copy = pltpu.make_async_remote_copy(
                src_ref=source(d + 1),
                dst_ref=target,
                send_sem=send.at[at],
                recv_sem=recv.at[at],
                device_id=peer,
                device_id_type=MESH,
            )
            copy.start()
            copies.append(copy)
        pending.extend(copies)
        return copies

    def arrive(copies):
        for copy in copies:
            copy.wait_recv()

    for q in range(span_i // GROUP):
        pltpu.make_async_copy(
            t_ref.at[pl.ds(q * GROUP, GROUP)], t32.at[pl.ds(q * GROUP, GROUP)], t_sem.at[q]
        ).start()

    barrier = pltpu.get_barrier_semaphore()
    greeted = gx_peers + yc_peers
    for peer in greeted:
        pl.semaphore_signal(barrier, inc=1, device_id=peer, device_id_type=MESH)

    c_one[gy] = jnp.concatenate([fc_ref[...], fc_ref[...]], axis=1)
    b_one[gz] = jnp.concatenate([fb_ref[...], fb_ref[...]], axis=1)

    def split_tensor(q, _):
        rows = pl.ds(q * GROUP, GROUP)
        pltpu.make_async_copy(t_ref.at[rows], t32.at[rows], t_sem.at[q]).wait()

        def one(i, _):
            thi[i], tlo[i] = split(t32[i])
            return 0

        lax.fori_loop(q * GROUP, (q + 1) * GROUP, one, 0)
        return 0

    pl.semaphore_wait(barrier, len(greeted))

    c_first = start(gy_peers, lambda d: c_one.at[gy], c_one.at[gy])
    b_first = start(gz_peers, lambda d: b_one.at[gz], b_one.at[gz])
    lax.fori_loop(0, 2, split_tensor, 0)
    arrive(c_first)
    c_all[gx] = jnp.where(low((4, 128)), c_one[0], c_one[1])
    c_second = start(gx_peers, lambda d: c_all.at[gx], c_all.at[gx])
    arrive(b_first)
    b_all[gx] = jnp.concatenate(
        [jnp.where(low((6, 128)), b_one[0], b_one[2]), jnp.where(low((6, 128)), b_one[1], b_one[3])],
        axis=0,
    )
    b_second = start(gx_peers, lambda d: b_all.at[gx], b_all.at[gx])
    lax.fori_loop(2, span_i // GROUP, split_tensor, 0)

    arrive(c_second)
    pieces = []
    for g in range(16):
        piece = c_all[g]
        other = swap(piece)
        side = low((4, 128))
        pieces += [jnp.where(side, piece, other), jnp.where(side, other, piece)]
    block_c = jnp.concatenate(pieces, axis=0)
    gram_c = matmul(block_c.T, block_c)[:RANK]
    gc_slots[gz] = compact(gram_c)
    gc_copies = start(gz_peers, lambda d: gc_slots.at[gz], gc_slots.at[gz])
    c_high, c_low = split(block_c)
    side = low((128, 128))
    none = jnp.zeros((128, 128), BF16)
    weights[:128, :128] = jnp.where(side, c_high, none)
    weights[:128, 128:] = jnp.where(side, c_low, none)
    weights[128:, :128] = jnp.where(side, none, c_high)
    weights[128:, 128:] = jnp.where(side, none, c_low)

    half_j = along.shape[1]

    def along_step(q, _):
        rows = pl.ds(q * GROUP, GROUP)

        def wide(ref):
            left, right = ref[rows, :half_j, :], ref[rows, half_j:, :]
            return jnp.concatenate([left, right], axis=2).reshape(GROUP * half_j, 256)

        both = jnp.dot(wide(thi), weights[...], preferred_element_type=F32)
        rest = jnp.dot(wide(tlo), weights[:, :128], preferred_element_type=F32)
        total = both[:, :128] + (both[:, 128:] + rest)
        along[rows] = total.reshape(GROUP, half_j, 128)
        return 0

    lax.fori_loop(0, span_i // GROUP, along_step, 0)

    arrive(b_second)
    for g in range(8):
        one, two = b_all[g], b_all[g + 8]
        side = low((12, 128))
        b_packed[24 * g : 24 * g + 12, :] = jnp.where(side, one, swap(two))
        b_packed[24 * g + 12 : 24 * g + 24, :] = jnp.where(side, swap(one), two)
    block_b = b_packed[...]

    def moment_a(i, _):
        product = along[i] * block_b
        ma_part[i] = jnp.sum(product.reshape(half_j // 8, 8, 128), axis=0)
        return 0

    lax.fori_loop(0, span_i, moment_a, 0)
    ma_slots[yc_me] = compact(fold(jnp.sum(ma_part[...], axis=1)))
    ma_copies = start(yc_peers, lambda d: ma_slots.at[yc_me], ma_slots.at[yc_me])
    gb_slots[gy] = compact(gram_packed(block_b))
    gb_copies = start(gy_peers, lambda d: gb_slots.at[gy], gb_slots.at[gy])
    arrive(gc_copies)
    arrive(gb_copies)
    gram_c = expand(gc_slots[0] + gc_slots[1] + gc_slots[2] + gc_slots[3])
    gram_b = expand(gb_slots[0] + gb_slots[1])
    inverse_a = block_diagonal(inverse(gram_b * gram_c))
    arrive(ma_copies)
    moment = ma_slots[0]
    for g in range(1, 8):
        moment = moment + ma_slots[g]
    ua = matmul(moment, inverse_a)
    ua_slots[gx] = ua
    ua_copies = start(gx_peers, lambda d: ua_slots.at[gx], ua_slots.at[gx])

    ua_rows[...] = expand(ua)

    def moment_b(i, total):
        return total + along[i] * ua_rows[pl.ds(i, 1), :]

    moment = lax.fori_loop(0, span_i, moment_b, jnp.zeros((half_j, 128), F32), unroll=4)
    mb_part[...] = moment.reshape(mb_part.shape)
    mb_slots[xc_me] = mb_part[xc_me]
    mb_copies = start(xc_peers, lambda d: mb_part.at[lax.rem(xc_me + d, 8)], mb_slots.at[xc_me])
    arrive(mb_copies)
    moment = mb_slots[0]
    for g in range(1, 8):
        moment = moment + mb_slots[g]
    mb_sum[zh_me] = moment
    mb_copies = start(zh_peers, lambda d: mb_sum.at[zh_me], mb_sum.at[zh_me])
    arrive(ua_copies)
    gram_ua = gram_packed(ua_slots[...].reshape(256, 128))
    scale_a, scale_a_down = scale_rows(gram_ua, float(span_i * 16))
    gram_a = gram_ua / (scale_a * scale_a_down)
    inverse_b = block_diagonal(inverse(gram_a * gram_c))
    shard_a = ua_slots[gx] / scale_a
    full_a = expand(shard_a)
    turned = jnp.concatenate([full_a, full_a, full_a, full_a], axis=0).T
    for i in range(32):
        a_columns[i] = jnp.broadcast_to(turned[:RANK, i : i + 1], (RANK, 128))
    picked = jnp.where(gy == 0, shard_a, swap(shard_a))
    ua_rows[:16, :] = picked
    a_ref[...] = ua_rows[pl.ds(gz * 4, 4), :][:, :RANK]
    arrive(mb_copies)
    moment = mb_sum[0]
    for g in range(1, 8):
        moment = moment + mb_sum[g]
    ub[xc_me] = matmul(moment / scale_a, inverse_b)
    ub_copies = start(xc_peers, lambda d: ub.at[xc_me], ub.at[xc_me])
    arrive(ub_copies)

    block_b = ub[...].reshape(half_j, 128)
    gu_slots[gy] = compact(gram_packed(block_b))
    gu_copies = start(gy_peers, lambda d: gu_slots.at[gy], gu_slots.at[gy])
    turned = block_b.T
    turned_high, turned_low = split(turned)
    left = [
        jnp.concatenate([turned_high[h * RANK : (h + 1) * RANK], turned_low[h * RANK : (h + 1) * RANK]], axis=0)
        for h in range(2)
    ]
    left = jnp.concatenate(left, axis=1)

    def moment_c(i, total):
        right = jnp.concatenate([thi[i], tlo[i]], axis=1)
        part = jnp.dot(left, right, preferred_element_type=F32)
        part = part[:RANK, :128] + (part[:RANK, 128:] + part[RANK:, :128])
        return total + part * a_columns[i]

    moment = lax.fori_loop(0, span_i, moment_c, jnp.zeros((RANK, 128), F32), unroll=2)
    moment = compact(jnp.concatenate([moment, moment], axis=0).T)
    for p in range(4):
        mc_part[p, :8, :] = moment[p * 8 : p * 8 + 8]
        mc_part[p, 8:, :] = moment[32 + p * 8 : 32 + p * 8 + 8]
    mc_slots[x] = mc_part[x]
    mc_copies = start(xx_peers, lambda d: mc_part.at[lax.rem(x + d, 4)], mc_slots.at[x])
    arrive(gu_copies)
    gram_ub = expand(gu_slots[0] + gu_slots[1])
    scale_b, scale_b_down = scale_rows(gram_ub, float(half_j * 4))
    gram_b = gram_ub / (scale_b * scale_b_down)
    arrive(mc_copies)
    mc_sum[zl_me] = mc_slots[0] + mc_slots[1] + (mc_slots[2] + mc_slots[3])
    mc_copies = start(zl_peers, lambda d: mc_sum.at[zl_me], mc_sum.at[zl_me])
    inverse_c = block_diagonal(inverse(gram_a * gram_b))
    shard_b = block_b / scale_b
    b_packed[...] = jnp.where(z // 2 == 0, shard_b, swap(shard_b))
    first = lax.rem(z, 2) * 96 + x * 24 + yh * 12 + core * 6
    b_ref[...] = b_packed[pl.ds(first, 6), :][:, :RANK]
    arrive(mc_copies)
    moment = mc_sum[0]
    for g in range(1, 8):
        moment = moment + mc_sum[g]
    uc = matmul(moment / scale_b, inverse_c)
    ss_slots[xg_me] = fold(jnp.sum(uc * uc, axis=0, keepdims=True))
    ss_copies = start(xg_peers, lambda d: ss_slots.at[xg_me], ss_slots.at[xg_me])
    picked = jnp.where(z // 2 == 0, uc, swap(uc))
    arrive(ss_copies)
    total = jnp.sum(ss_slots[...], axis=0)
    scale_c = jnp.sqrt(total / float(128 * 4) + 1e-06)
    ua_rows[:16, :] = picked / scale_c
    c_ref[...] = ua_rows[pl.ds(lax.rem(z, 2) * 8 + gy * 4, 4), :][:, :RANK]

    for copy in pending:
        copy.wait_send()


COPIES = 1 + 3 + 15 + 15 + 3 + 7 + 1 + 15 + 7 + 7 + 7 + 1 + 3 + 7 + 15


def local(tensor, factor_b, factor_c):
    span_i, span_j, span_k = tensor.shape
    half_j = span_j // 2
    vmem = pl.BlockSpec(memory_space=pltpu.VMEM)
    scratch = [
        pltpu.VMEM(tensor.shape, F32),
        pltpu.VMEM(tensor.shape, BF16),
        pltpu.VMEM(tensor.shape, BF16),
        pltpu.VMEM((span_i, half_j, 128), F32),
        pltpu.VMEM((256, 256), BF16),
        pltpu.VMEM((2, 4, 128), F32),
        pltpu.VMEM((16, 4, 128), F32),
        pltpu.VMEM((4, 6, 128), F32),
        pltpu.VMEM((16, 12, 128), F32),
        pltpu.VMEM((half_j, 128), F32),
        pltpu.VMEM((2, 32, 128), F32),
        pltpu.VMEM((4, 32, 128), F32),
        pltpu.VMEM((span_i, 8, 128), F32),
        pltpu.VMEM((8, 16, 128), F32),
        pltpu.VMEM((16, 16, 128), F32),
        pltpu.VMEM((32, 128), F32),
        pltpu.VMEM((32, RANK, 128), F32),
        pltpu.VMEM((8, 24, 128), F32),
        pltpu.VMEM((8, 24, 128), F32),
        pltpu.VMEM((8, 24, 128), F32),
        pltpu.VMEM((8, 24, 128), F32),
        pltpu.VMEM((2, 32, 128), F32),
        pltpu.VMEM((4, 16, 128), F32),
        pltpu.VMEM((4, 16, 128), F32),
        pltpu.VMEM((8, 16, 128), F32),
        pltpu.VMEM((16, 1, 128), F32),
        pltpu.SemaphoreType.DMA((span_i // GROUP,)),
        pltpu.SemaphoreType.DMA((COPIES,)),
        pltpu.SemaphoreType.DMA((COPIES,)),
    ]
    return pl.pallas_call(
        kernel,
        out_shape=(
            jax.ShapeDtypeStruct((4, RANK), F32),
            jax.ShapeDtypeStruct((6, RANK), F32),
            jax.ShapeDtypeStruct((4, RANK), F32),
        ),
        in_specs=[pl.BlockSpec(memory_space=pl.ANY), vmem, vmem],
        out_specs=(vmem, vmem, vmem),
        scratch_shapes=scratch,
        compiler_params=pltpu.CompilerParams(
            collective_id=0, has_side_effects=True, vmem_limit_bytes=48 * 1024 * 1024
        ),
    )(tensor, factor_b, factor_c)


def solution(mesh):
    return jax.shard_map(
        local,
        mesh=mesh,
        in_specs=(P("gx", "gy", "gz"), P(("gy", "gx", "gz"), None), P(("gz", "gx", "gy"), None)),
        out_specs=(
            P(("gx", "gy", "gz"), None),
            P(("gy", "gx", "gz"), None),
            P(("gz", "gx", "gy"), None),
        ),
        check_vma=False,
    )
```

time: 1370 us -> 61.5 us (0.04)
  blocking collectives: 713 us -> 0 us
  waiting for transfers between devices: 524 us -> 0 us
  matrix products: 64.9 us -> 0 us
  Pallas kernels: 0 us -> 57.6 us
  other arithmetic: 38.3 us -> 0 us
  between operations: 16.5 us -> 0.65 us
    unnamed x2 -> x0, waiting for transfers between devices: 524 us -> none
    psum x4 -> x0, blocking collectives: 287 us -> none  [the longest x3 218 us: local(): gram_raw = lax.psum(gram_of(unscaled), ('gx', 'gy', 'gz'))]
    all_gather x4 -> x0, blocking collectives: 276 us -> none  [the longest x1 107 us: local(): block_b = lax.all_gather(factor_b, ('gx', 'gz'), axis=0, tiled=True)]
    unnamed x2 -> x0, blocking collectives: 150 us -> none
    dot_general x10 -> x0, matrix products: 62.7 us -> none  [the longest x1 21.7 us: local(): jnp.einsum('rjk,jr->kr', window, block_b, precision=HIGHEST_PRECISION)]
    pallas_call x0 -> x1, Pallas kernels: none -> 57.6 us  [local(): pl.pallas_call(kernel, out_shape=(jax.ShapeDtypeStruct((4, RANK), F32), j...]
    another operation x15 -> x0, other arithmetic: 36.2 us -> none  [the longest x9 19.6 us: solve_rows(): lower = jnp.linalg.cholesky(system)]
  transfers between devices with their start and end apart: 1 -> 0, of which waited for: 1 -> 0; matrix products, arithmetic and copies ran while one was open for 3% -> 0% of each run, Pallas kernels for 0% -> 0%
where the time goes in v1:
time: 61.5 us; the launch traced here: 61.4 us
  Pallas kernels  57.6 us (94%)
  local copies, waits for them, and re-layouts  3.11 us (5%)
  between operations  0.65 us (1%)
    pallas_call x1, Pallas kernels, local(): pl.pallas_call(kernel, out_shape=(jax.ShapeDtypeStruct((4, RANK), F32), j...  57.6 us
    unnamed x7, local copies, waits for them, and re-layouts  3.11 us

profile of v1, /device:TPU:1, one launch (start us, length us, event | category | flops | bytes accessed | tf_op | source)
XLA Modules:
  0.0 61.4 jit_solution(542224263992034946)
XLA Ops:
  0.6 0.0 copy-start
  0.6 0.7 %copy-done = f32[6,64]{1,0:T(8,128)S(1)} copy-done((f32[6,64]{1,0:T(8,128)S(1)}, f32[6,64]{1,0:T(8,128)}, u32[]{:S(2)}) %copy-start) | copy-done | bytes 1560
  1.3 0.0 copy-start.1
  1.3 0.7 %copy-done.1 = f32[4,64]{1,0:T(4,128)S(1)} copy-done((f32[4,64]{1,0:T(4,128)S(1)}, f32[4,64]{1,0:T(4,128)}, u32[]{:S(2)}) %copy-start.1) | copy-done | bytes 1048
  2.0 57.6 %shard_map.58 = (f32[4,64]{1,0:T(4,128)S(1)}, f32[6,64]{1,0:T(8,128)S(1)}, f32[4,64]{1,0:T(4,128)S(1)}) custom-call(f32[32,384,128]{2,1,0:T(8,128)} %t_ref.1, f32[6,64]{1,0:T(8,128)S(1)} %copy-done, f32[4,64]{1,0:T(4,128)S(1)} %copy-done.1), custom_call_target="tpu_custom_call" | custom-call | tf_op jit(solution)/shard_map/pallas_call | solution.py:381
  59.6 0.6 copy.9
  60.2 0.6 copy.10
  60.8 0.6 copy.11
Async XLA Ops:
  0.6 0.7 %copy-start = (f32[6,64]{1,0:T(8,128)S(1)}, f32[6,64]{1,0:T(8,128)}, u32[]{:S(2)}) copy-start(f32[6,64]{1,0:T(8,128)} %fb_ref.1) | copy-start | bytes 4612
  1.3 0.7 %copy-start.1 = (f32[4,64]{1,0:T(4,128)S(1)}, f32[4,64]{1,0:T(4,128)}, u32[]{:S(2)}) copy-start(f32[4,64]{1,0:T(4,128)} %fc_ref.1) | copy-start | bytes 3076
